TPU v7x, 32 devices: a whole 2x2x4 slice. The times are simulated.
32 devices in a mesh: noise: 2 (over y), patch: 16 (over z, x, core).
Axes of the slice: x: 2, y: 2, z: 4, core: 2. Of those that a mesh axis runs over, the one named last changes fastest.
Arguments:
- nodes: bfloat16 [2, 8192, 512], P('noise', 'patch'), may hold values from -6 to 6
- noise_level: float32 [2], P('noise'), may hold values from 0.03 to 80
- patch_sizes: int32 [16], P('patch'), may hold values from 256 to 512, as said below
- send_rows: int32 [2048], P('patch'), may hold values from 0 to 511, as said below
- neighbours: int32 [16, 8192], P(None, 'patch'), may hold values from 0 to 639, as said below
- qkv_weight: bfloat16 [2, 512, 1536], replicated, may hold values from -0.25 to 0.25
- out_weight: bfloat16 [2, 512, 512], replicated, may hold values from -0.5 to 0.5
- up_weight: bfloat16 [2, 512, 2048], replicated, may hold values from -0.25 to 0.25
- down_weight: bfloat16 [2, 2048, 512], replicated, may hold values from -0.125 to 0.125
- cond_weight: bfloat16 [2, 4, 32, 512], replicated, may hold values from -0.5 to 0.5
- cotangent: bfloat16 [2, 8192, 512], P('noise', 'patch'), may hold values from -6 to 6
Outputs:
- result: bfloat16 [2, 8192, 512], P('noise', 'patch')
- input_grad: float32 [2, 8192, 512], P('noise', 'patch')
- qkv_grad: float32 [2, 512, 1536], replicated
- out_grad: float32 [2, 512, 512], replicated
- up_grad: float32 [2, 512, 2048], replicated
- down_grad: float32 [2, 2048, 512], replicated
- cond_grad: float32 [2, 4, 32, 512], replicated
Inputs may be any that keep to these rules, and one draw needn't show every extreme that they name: `patch_sizes`: live rows of each patch, between half of 512 and 512; one patch has exactly 512, another exactly 256. `send_rows`: block p (128 entries) holds rows of patch p below its size; its first 64 go to the patch before, its last 64 to the patch after, the patches forming a loop. `neighbours`: an entry below 512 is a row of the node's own patch, from 512 to 575 one received from the patch before, above it one received from the patch after; a live node names only live rows of its patch or received rows; entry 0 is the node itself.
All inputs are finite; a program needn't handle non-finite values.
Results may differ from a plain program's by a relative error of at most 0.018.
Values may be sent and summed in bfloat16 or wider, within the bound.
A program may use at most 256 MiB of HBM per device.

v0:
```python
import functools

import jax
import jax.numpy as jnp
import numpy as np
from jax import lax
from jax.experimental import pallas as pl
from jax.experimental.pallas import tpu as pltpu
from jax.sharding import PartitionSpec as P

HEADS = 4
COND = 32
SLOTS = 16
EPSILON = 1e-05
LOG2E = 1.4426950408889634
MESH = pl.DeviceIdType.MESH
F32 = jnp.float32
BF16 = jnp.bfloat16
BLOCK = 512


WHOLE, LEFT, RIGHT = (0, BLOCK), (0, BLOCK // 2), (BLOCK // 2, BLOCK // 2)


def square(row, size, x, y, last):
    one, two = size // 2, size // 4
    first = [(row + x * one, row + (1 - x) * one, one, LEFT, LEFT, 0, LEFT, "x")]
    second = []
    for i in range(2):
        at = row + i * one
        first.append((at + y * two, at + (1 - y) * two, two, RIGHT, RIGHT, i * two, RIGHT, "y"))
        if last:
            second.append((at + y * two, at + y * two, two, RIGHT, RIGHT, i * two, RIGHT, "x"))
    mine = row + x * one
    kept = mine + y * two
    if last:
        second.append((mine, mine, one, LEFT, LEFT, 0, LEFT, "y"))
    else:
        second.append((kept, mine + (1 - y) * two, two, LEFT, LEFT, 0, LEFT, "y"))
        other = row + (1 - x) * one + y * two
        second.append((kept, other, two, RIGHT, RIGHT, 0, RIGHT, "x"))
    return kept, two, first, second


def along_line(row, size, cols, bit, b, last):
    if last:
        return (row, size, cols), [(row, row, size, cols, cols, 0, (0, cols[1]), b)]
    if size >= 32:
        size //= 2
        keep, send = row + bit * size, row + (1 - bit) * size
        return (keep, size, cols), [(keep, send, size, cols, cols, 0, (0, cols[1]), b)]
    first, width = cols[0], cols[1] // 2
    keep, send = (first + bit * width, width), (first + (1 - bit) * width, width)
    return (row, size, keep), [(row, row, size, keep, send, 0, (0, width), b)]


def exchanges(core, x, y, bits, line_first):
    half = BLOCK // 2
    row, size, cols = core * half, half, WHOLE
    out = [[(row, (1 - core) * half, half, WHOLE, WHOLE, 0, WHOLE, "core")]]
    if not line_first:
        row, size, first, second = square(row, size, x, y, False)
        out += [first, second]
    for b, bit in enumerate(bits):
        last = not line_first and b == len(bits) - 1
        (row, size, cols), parts = along_line(row, size, cols, bit, b, last)
        out.append(parts)
    if line_first:
        row, size, first, second = square(row, size, x, y, True)
        out += [first, second]
    return out


LINE_FIRST = (4, 13, 16, 21)


def goes_line_first(n, line_bits):
    return line_bits == 2 and n in LINE_FIRST


MADE = {
    **{f"down{f}": f for f in range(4)},
    **{f"up{f}": 4 + f for f in range(4)},
    **{"out": 8, "query": 9, "key": 10, "value": 11},
}
LAYER_PIECES = (
    (
        "down0", "down1", "feed0", "down2", "feed1", "down3", "feed2", "feed3", "up0", "norm2", "attended",
        "up3", "head0", "up1", "head1", "halo0", "head2", "head3", "halo1", "up2", "out", "query", "table",
        "key", "value", "norm1",
    ),
    (
        "down0", "down1", "down2", "feed0", "feed1", "feed2", "down3", "feed3", "norm2", "up2", "attended",
        "head0", "up1", "head1", "halo0", "up0", "head2", "head3", "up3", "halo1", "query", "out", "table",
        "key", "value", "norm1",
    ),
)

REDUCE_LAGS = ((1, 3, 2, 3, 4), (1, 4, 4, 3, 2))
GATHER_LAGS = ((3, 3, 7, 3), (2, 4, 7, 5))
GATHER_WAIT = (1, 1)
SUMS_LAG = 3


def schedule(line_bits, slots):
    tables = [exchanges(0, 0, 0, [0] * line_bits, f) for f in (False, True)]
    stages = 3 + line_bits
    sum_dirs = ["core", "x", *range(line_bits), "y"]

    def dirs_of(kind, s, n):
        if kind == "sums":
            return {sum_dirs[s]}
        return {p[7] for p in tables[goes_line_first(n, line_bits)][s]}

    order, sent, seen = [], [], set()
    reduced = {}
    places = {}

    def told(since, dirs):
        return all(
            any(at > since and d in ds and key in seen for at, ds, key in sent) for d in dirs
        )

    def find_slot(kind, s, dirs):
        for slot in range(slots):
            since = places.get((kind, s, slot), -1)
            if since == -1 or (since is not None and told(since, dirs)):
                return slot
        return None

    def lag(kind, s, n):
        if kind == "sums":
            return SUMS_LAG
        lags = (REDUCE_LAGS if kind == "reduce" else GATHER_LAGS)[goes_line_first(n, line_bits)]
        if kind == "reduce":
            return lags[min(s, len(lags) - 1)]
        return lags[max(0, len(lags) - 1 - s)]

    flying, waiting = [], []

    def start_due(turn):
        for item in sorted(v for v in waiting if v[0] <= turn):
            _, kind, s, n = item
            dirs = dirs_of(kind, s, n)
            if kind == "gather" and not told(reduced[s, n], dirs):
                continue
            slot = 0 if kind == "sums" else find_slot(kind, s, dirs)
            if slot is None:
                continue
            waiting.remove(item)
            order.append(("send", kind, s, n, slot))
            places[kind, s, slot] = None
            sent.append((len(order), dirs, (kind, s, n)))
            flying.append((turn + lag(kind, s, n), kind, s, n, slot))

    def take_turn(turn):
        due = [v for v in flying if v[0] <= turn]
        rank = {"gather": 0, "sums": 1, "reduce": 2}
        due.sort(key=lambda v: (rank[v[1]], v[2] if v[1] == "gather" else -v[2], v[3]))
        for item in due:
            flying.remove(item)
            _, kind, s, n, slot = item
            order.append(("take", kind, s, n, slot))
            seen.add((kind, s, n))
            places[kind, s, slot] = len(order)
            if kind == "reduce":
                reduced[s, n] = len(order)
                if s + 1 < stages:
                    waiting.append((turn, kind, s + 1, n))
                else:
                    wait = GATHER_WAIT[goes_line_first(n, line_bits)]
                    waiting.append((turn + wait, "gather", s - 1, n))
            elif kind == "gather" and s > 0:
                waiting.append((turn, kind, s - 1, n))
            elif kind == "sums" and s + 1 < len(sum_dirs):
                waiting.append((turn, kind, s + 1, n))
            start_due(turn)
        start_due(turn)

    turn = 0
    for i in range(2):
        for name in LAYER_PIECES[i]:
            order.append(("work", name, i))
            if name in MADE:
                waiting.append((turn, "reduce", 0, i * 12 + MADE[name]))
                take_turn(turn)
                turn += 1
    waiting.append((turn, "sums", 0, 0))
    while flying or waiting:
        before = len(order)
        take_turn(turn)
        turn += 1
        if len(order) == before and not flying:
            for d in dirs_of(*waiting[0][1:]):
                order += [("send", "token", d, 0, 0), ("take", "token", d, 0, 0)]
                sent.append((len(order), {d}, ("token", len(order))))
                seen.add(("token", len(order)))
    return order


def nn(a, b):
    return lax.dot_general(a, b, (((1,), (0,)), ((), ())), preferred_element_type=F32)


def nt(a, b):
    return lax.dot_general(a, b, (((1,), (1,)), ((), ())), preferred_element_type=F32)


def tn(a, b):
    return lax.dot_general(a, b, (((0,), (0,)), ((), ())), preferred_element_type=F32)


def mega(
    patches,
    order,
    noise_ref,
    sizes_ref,
    send_ref,
    nbr_ref,
    cond_w_ref,
    freq_ref,
    nodes_hbm,
    qkv_hbm,
    out_hbm,
    up_hbm,
    down_hbm,
    cot_hbm,
    result_ref,
    igrad_ref,
    cond_grad_ref,
    w,
    logc,
    sel,
    sel_t,
    cond,
    hid,
    mid,
    xh1,
    xh2,
    rs1,
    rs2,
    act1,
    act2,
    low,
    tr,
    qv,
    kv,
    prob,
    att_t,
    gate,
    slope,
    dob,
    dkv,
    dqkv,
    rim,
    rin,
    node_in,
    cot_in,
    sums,
    stat,
    sums_in,
    load_sem,
    halo_send,
    halo_recv,
    rs_send,
    rs_recv,
    ag_send,
    ag_recv,
    sum_send,
    sum_recv,
    token,
    *inbox,
):
    rows = hid.shape[0]
    table = kv.shape[1]
    halo = rim.shape[0] // 2
    my_noise = lax.axis_index("noise")
    me = lax.axis_index("patch")
    before = (my_noise, lax.rem(me + patches - 1, patches))
    after = (my_noise, lax.rem(me + 1, patches))

    def place(t, k, down, up, out, qkv):
        if k < 4:
            return down.at[t, pl.ds(k * BLOCK, BLOCK), :]
        if k < 8:
            return up.at[t, :, pl.ds((k - 4) * BLOCK, BLOCK)]
        if k < 9:
            return out.at[t]
        return qkv.at[t, :, pl.ds((k - 9) * BLOCK, BLOCK)]

    def load(t, k):
        src = place(t, k, down_hbm, up_hbm, out_hbm, qkv_hbm)
        return pltpu.make_async_copy(src, w.at[(1 - t) * 12 + k], load_sem.at[t])

    node_copy = pltpu.make_async_copy(nodes_hbm.at[0], node_in, load_sem.at[2])
    cot_copy = pltpu.make_async_copy(cot_hbm.at[0], cot_in, load_sem.at[3])
    node_copy.start()
    for t in range(2):
        for k in (9, 10, 11, 8, 4, 0, 5, 1, 6, 2, 7, 3):
            load(t, k).start()
    cot_copy.start()

    core = lax.rem(me, 2)
    x = lax.rem(me // 2, 2)
    y = my_noise
    z = me // 4
    line = patches // 4
    core_peer = (my_noise, me + 1 - 2 * core)
    x_peer = (my_noise, me + 2 - 4 * x)
    y_peer = (1 - my_noise, me)

    barrier = pltpu.get_barrier_semaphore()
    greeted = [before, after, core_peer, x_peer, y_peer]
    for b in range(line.bit_length() - 1):
        bit = lax.rem(z // (1 << b), 2)
        greeted.append((my_noise, me + 4 * (1 << b) * (1 - 2 * bit)))
    for other in greeted:
        pl.semaphore_signal(barrier, inc=1, device_id=other, device_id_type=MESH)

    step_rows = 64

    def count(i, _):
        base = i * step_rows
        ids = lax.broadcasted_iota(jnp.int32, (step_rows, rows), 0) + base
        total = jnp.zeros((step_rows, rows), F32)
        for j in range(nbr_ref.shape[0]):
            total = total + jnp.where(nbr_ref[j : j + 1, :] == ids, 1.0, 0.0)
        logc[pl.ds(base, step_rows), :] = jnp.where(total > 0.0, jnp.log(total) * LOG2E, -1e30)
        return 0

    lax.fori_loop(0, table // step_rows, count, 0)
    picked = jnp.where(
        lax.broadcasted_iota(jnp.int32, (rows, 2 * halo), 0) == send_ref[...], 1.0, 0.0
    )
    sel_t[...] = picked.astype(BF16)
    sel[...] = picked.T.astype(BF16)

    def features(noise):
        phase = jnp.log(noise) * freq_ref[...]
        is_sin = lax.broadcasted_iota(jnp.int32, (COND, 128), 0) < COND // 2
        feats = jnp.where(is_sin, jnp.sin(phase), jnp.cos(phase))
        return jnp.concatenate([feats] * (hid.shape[1] // 128), axis=1)

    wide = features(jnp.broadcast_to(noise_ref[...], (COND, 128)))
    sums[8:16, :] = jnp.broadcast_to(noise_ref[...], (8, hid.shape[1]))
    for t in range(2):
        for i in range(4):
            cond[t * 4 + i] = jnp.sum(cond_w_ref[t, i].astype(F32) * wide, 0, keepdims=True)

    node_copy.wait()
    hid[...] = node_in[...].astype(F32)
    pl.semaphore_wait(barrier, len(greeted))

    head = hid.shape[1] // HEADS
    unit = LOG2E * head ** (-0.5)
    ln_rows = 64

    def norm(value_ref, t, first, normed_ref, inv_ref, out_ref):
        def body(i, _):
            at = pl.ds(i * ln_rows, ln_rows)
            value = value_ref[at, :]
            centred = value - jnp.mean(value, -1, keepdims=True)
            inv = lax.rsqrt(jnp.mean(centred * centred, -1, keepdims=True) + EPSILON)
            normed = centred * inv
            normed_ref[t, at, :] = normed
            inv_ref[t, at, :] = inv
            out_ref[t, at, :] = (
                normed * (1.0 + cond[t * 4 + first]) + cond[t * 4 + first + 1]
            ).astype(BF16)
            return 0

        lax.fori_loop(0, rows // ln_rows, body, 0, unroll=4)

    def halo_copies(stage, part, src, dst, to_before, to_after):
        cols = pl.ds(part * BLOCK, BLOCK)
        return [
            pltpu.make_async_remote_copy(
                src_ref=src.at[pl.ds(i * halo, halo), cols],
                dst_ref=dst.at[pl.ds(row, halo), cols],
                send_sem=halo_send.at[stage * 2 + part, i],
                recv_sem=halo_recv.at[stage * 2 + part, i],
                device_id=other,
                device_id_type=MESH,
            )
            for i, (row, other) in enumerate(((to_before, before), (to_after, after)))
        ]

    def forward(t, _):
        base = (1 - t) * 12
        layer = w.at[pl.ds(base, 12)]
        pltpu.make_async_copy(layer, layer, load_sem.at[t]).wait()
        norm(hid, t, 0, xh1, rs1, act1)
        a = act1[t]
        copies = []
        for part in range(2):
            cols = pl.ds(part * BLOCK, BLOCK)
            kv[t, pl.ds(0, rows), cols] = nn(a, w[base + 10 + part]).astype(BF16)
            rim[:, cols] = nn(sel[...], kv[t, pl.ds(0, rows), cols]).astype(BF16)
            copies.append(halo_copies(t, part, rim, kv.at[t], rows + halo, rows))
            for copy in copies[part]:
                copy.start()
        qv[t] = nn(a, w[base + 9]).astype(BF16)
        own, far = pl.ds(0, rows), pl.ds(rows, table - rows)
        for h in range(HEADS):
            lanes = pl.ds(h * head, head)
            for c in range(2):
                cols = pl.ds(c * 256, 256)
                score = nt(kv[t, own, lanes], qv[t, cols, lanes]) * unit + logc[own, cols]
                top = jnp.max(score, 0, keepdims=True)
                part = jnp.exp2(score - top)
                prob[t, h, own, cols] = part.astype(BF16)
                stat[2 * h : 2 * h + 1, cols] = top
                stat[2 * h + 1 : 2 * h + 2, cols] = jnp.sum(part, 0, keepdims=True)
        for copy in copies[0]:
            copy.wait()
        for h in range(HEADS):
            lanes = pl.ds(h * head, head)
            score = nt(kv[t, far, lanes], qv[t, :, lanes]) * unit + logc[far, :]
            near_top = stat[2 * h : 2 * h + 1, :]
            top = jnp.maximum(near_top, jnp.max(score, 0, keepdims=True))
            part = jnp.exp2(score - top)
            scale = jnp.exp2(near_top - top)
            inv = 1.0 / (stat[2 * h + 1 : 2 * h + 2, :] * scale + jnp.sum(part, 0, keepdims=True))
            prob[t, h, far, :] = (part * inv).astype(BF16)
            prob[t, h, own, :] = (prob[t, h, own, :].astype(F32) * (scale * inv)).astype(BF16)
        for copy in copies[1]:
            copy.wait()
        for h in range(HEADS):
            lanes = pl.ds(h * head, head)
            values = kv[t, :, pl.ds(BLOCK + h * head, head)]
            att_t[t, lanes, :] = tn(values, prob[t, h]).astype(BF16)
        mid[...] = hid[...] + tn(att_t[t], w[base + 8])
        norm(mid, t, 2, xh2, rs2, act2)
        for f in range(4):
            u = nn(act2[t], w[base + 4 + f])
            sig = 0.5 * jnp.tanh(0.5 * u) + 0.5
            g = u * sig
            gate[t, f] = g.astype(BF16)
            slope[t, f] = (sig + g * (1.0 - sig)).astype(BF16)
            if f == 0:
                hid[...] = mid[...] + nn(gate[t, f], w[base + f])
            else:
                hid[...] += nn(gate[t, f], w[base + f])
        return 0

    lax.fori_loop(0, 2, forward, 0)

    cot_copy.wait()

    def turn(i, _):
        at = pl.ds(i * ln_rows, ln_rows)
        ids = lax.broadcasted_iota(jnp.int32, (ln_rows, hid.shape[1]), 0) + i * ln_rows
        live = ids < sizes_ref[...]
        result_ref[0, at, :] = jnp.where(live, hid[at, :], 0.0).astype(BF16)
        hid[at, :] = jnp.where(live, cot_in[at, :].astype(F32), 0.0)
        return 0

    lax.fori_loop(0, rows // ln_rows, turn, 0)

    def norm_back(t, first, grad_ref, normed_ref, inv_ref, add_ref, out_ref):
        def body(i, carry):
            scale_sum, shift_sum = carry
            at = pl.ds(i * ln_rows, ln_rows)
            grad = grad_ref[at, :]
            normed = normed_ref[t, at, :]
            back = grad * normed
            scale_sum = scale_sum + jnp.sum(back.reshape(-1, 8, hid.shape[1]), 0)
            shift_sum = shift_sum + jnp.sum(grad.reshape(-1, 8, hid.shape[1]), 0)
            scaled = grad * (1.0 + cond[t * 4 + first])
            one = jnp.mean(scaled, -1, keepdims=True)
            two = jnp.mean(scaled * normed, -1, keepdims=True)
            out = add_ref[at, :] + inv_ref[t, at, :] * (scaled - one - normed * two)
            out_ref[at, :] = out
            low[at, :] = out.astype(BF16)
            return scale_sum, shift_sum

        zero = jnp.zeros((8, hid.shape[1]), F32)
        scale_sum, shift_sum = lax.fori_loop(0, rows // ln_rows, body, (zero, zero), unroll=4)
        sums[pl.ds(t * 4 + first, 1), :] = jnp.sum(scale_sum, 0, keepdims=True)
        sums[pl.ds(t * 4 + first + 1, 1), :] = jnp.sum(shift_sum, 0, keepdims=True)

    bits = [lax.rem(z // (1 << b), 2) for b in range(line.bit_length() - 1)]
    stages = 3 + len(bits)
    plans = [exchanges(core, x, y, bits, f) for f in (False, True)]
    peers = {"core": core_peer, "x": x_peer, "y": y_peer}
    for b, bit in enumerate(bits):
        peers[b] = (my_noise, me + 4 * (1 << b) * (1 - 2 * bit))

    def parts_of(s, n):
        return plans[goes_line_first(n, len(bits))][s]

    def box(row, size, cols):
        at = pl.ds(row if isinstance(row, int) else pl.multiple_of(row, 16), size)
        first = cols[0] if isinstance(cols[0], int) else pl.multiple_of(cols[0], 128)
        return at, pl.ds(first, cols[1])

    def copy_to(d, src, dst, pair):
        pltpu.make_async_remote_copy(
            src_ref=src,
            dst_ref=dst,
            send_sem=pair[0],
            recv_sem=pair[1],
            device_id=peers[d],
            device_id_type=MESH,
        ).start()

    def pair_of(kind, s, slot):
        if kind == "reduce":
            return rs_send.at[s, slot], rs_recv.at[s, slot]
        return ag_send.at[s, slot], ag_recv.at[s, slot]

    def send_block(kind, s, n, slot):
        pair = pair_of(kind, s, slot)
        for keep, send, size, cols, sent_cols, at, at_cols, d in parts_of(s, n):
            if kind == "reduce":
                copy_to(
                    d, w.at[n, *box(send, size, sent_cols)], inbox[s].at[slot, *box(at, size, at_cols)], pair
                )
            else:
                own = w.at[n, *box(keep, size, cols)]
                copy_to(d, own, own, pair)

    def settle(like, pair):
        for sem in pair:
            pltpu.make_async_copy(like, like, sem).wait()

    def take_block(kind, s, n, slot):
        settle(inbox[s].at[slot if kind == "reduce" else 0], pair_of(kind, s, slot))
        if kind == "reduce":
            for keep, _, size, cols, _, at, at_cols, _ in parts_of(s, n):
                step = min(size, 32)

                def add(i, _, keep=keep, cols=cols, at=at, at_cols=at_cols, step=step):
                    mine = (n, *box(keep + i * step, step, cols))
                    got = inbox[s][slot, *box(at + i * step, step, at_cols)]
                    w[mine] = (w[mine].astype(F32) + got.astype(F32)).astype(BF16)
                    return 0

                lax.fori_loop(0, size // step, add, 0)

    sum_dirs = ["core", "x", *range(len(bits)), "y"]

    def sum_rows(s):
        return pl.ds(0, 8 if s + 1 < len(sum_dirs) else 16)

    def send_sums(s):
        src, dst = sums.at[sum_rows(s)], sums_in.at[s, sum_rows(s)]
        copy_to(sum_dirs[s], src, dst, (sum_send.at[s], sum_recv.at[s]))

    def take_sums(s):
        settle(sums_in.at[s, sum_rows(s)], (sum_send.at[s], sum_recv.at[s]))
        if s + 1 < len(sum_dirs):
            sums[0:8, :] = sums[0:8, :] + sums_in[s, 0:8, :]

    low[...] = hid[...].astype(BF16)

    def pieces_of(i):
        t = 1 - i
        base = i * 12
        work = {}

        def down(f):
            slope[t, f] = (nt(low[...], w[base + f]) * slope[t, f].astype(F32)).astype(BF16)
            w[base + f] = tn(gate[t, f], low[...]).astype(BF16)

        def feed(f):
            if f == 0:
                tr[...] = act2[t].T
                mid[...] = nt(slope[t, f], w[base + 4 + f])
            else:
                mid[...] += nt(slope[t, f], w[base + 4 + f])

        def up(f):
            w[base + 4 + f] = nn(tr[...], slope[t, f]).astype(BF16)

        def attended():
            dob[...] = nt(low[...], w[base + 8]).astype(BF16)

        def head_back(h):
            lanes = pl.ds(h * head, head)
            keys = kv[t, :, lanes]
            values = kv[t, :, pl.ds(BLOCK + h * head, head)]
            weight = prob[t, h]
            grad_out = dob[:, lanes]
            grad_weight = nt(values, grad_out)
            spread = weight.astype(F32) * grad_weight
            delta = jnp.sum(spread, 0, keepdims=True)
            ds = (spread - weight.astype(F32) * delta).astype(BF16)
            dv = nn(weight, grad_out)
            dk = nn(ds, qv[t, :, lanes]) * (head ** (-0.5))
            dq_t = tn(keys, ds) * (head ** (-0.5))
            dqkv[:, lanes] = dq_t.T.astype(BF16)
            dkv[:, lanes] = dk[:rows]
            dkv[:, pl.ds(BLOCK + h * head, head)] = dv[:rows]
            first = (h // 2) * BLOCK + (h % 2) * head
            rim[:, pl.ds(first, head)] = dk[rows:].astype(BF16)
            rim[:, pl.ds(first + BLOCK // 2, head)] = dv[rows:].astype(BF16)

        copies = []

        def send_halo(part):
            copies.extend(halo_copies(2 + t, part, rim, rin.at[t], halo, 0))
            for copy in copies[-2:]:
                copy.start()

        def out():
            w[base + 8] = nn(att_t[t], low[...]).astype(BF16)

        def project(k):
            lanes = pl.ds(k * BLOCK, BLOCK)
            back = nt(dqkv[:, lanes], w[base + 9 + k])
            if k == 0:
                tr[...] = act1[t].T
                hid[...] = back
            else:
                hid[...] += back
            w[base + 9 + k] = nn(tr[...], dqkv[:, lanes]).astype(BF16)

        def whole_table():
            for copy in copies:
                copy.wait()
            for part in range(2):
                back = nn(sel_t[...], rin[t, :, pl.ds(part * BLOCK, BLOCK)])
                for i in range(2):
                    half = BLOCK // 2
                    first = i * BLOCK + part * half
                    total = dkv[:, pl.ds(first, half)] + back[:, i * half : (i + 1) * half]
                    dqkv[:, pl.ds(BLOCK + first, half)] = total.astype(BF16)

        for f in range(4):
            work[f"down{f}"] = functools.partial(down, f)
            work[f"feed{f}"] = functools.partial(feed, f)
            work[f"up{f}"] = functools.partial(up, f)
            work[f"head{f}"] = functools.partial(head_back, f)
        work["norm2"] = functools.partial(norm_back, t, 2, mid, xh2, rs2, hid, mid)
        work["attended"] = attended
        work["halo0"] = functools.partial(send_halo, 0)
        work["halo1"] = functools.partial(send_halo, 1)
        work["out"] = out
        work["query"] = functools.partial(project, 0)
        work["table"] = whole_table
        work["key"] = functools.partial(project, 1)
        work["value"] = functools.partial(project, 2)
        work["norm1"] = functools.partial(norm_back, t, 0, hid, xh1, rs1, mid, hid)
        return work

    layers = [pieces_of(0), pieces_of(1)]
    for act, *rest in order:
        if act == "work":
            name, i = rest
            layers[i][name]()
        else:
            kind, s, n, slot = rest
            if kind == "sums":
                (send_sums if act == "send" else take_sums)(s)
            elif kind == "token":
                if act == "send":
                    told = token.at[s if isinstance(s, int) else len(bits) + "xyc".index(s[0])]
                    pl.semaphore_signal(told, inc=1, device_id=peers[s], device_id_type=MESH)
                else:
                    pl.semaphore_wait(told, 1)
            else:
                (send_block if act == "send" else take_block)(kind, s, n, slot)

    igrad_ref[0] = hid[...]
    far_sums = len(sum_dirs) - 1
    other = features(jnp.concatenate([sums_in[far_sums, 8:16, 0:128]] * (COND // 8), axis=0))
    for t in range(2):
        for i in range(4):
            row = pl.ds(t * 4 + i, 1)
            cond_grad_ref[t, i] = wide * sums[row, :] + other * sums_in[far_sums, row, :]


def widen(
    result_in, igrad_in, cond_in, w, result, igrad, cond, qkv, out, up, down, stage, sems, small
):
    copies = [
        pltpu.make_async_copy(src, dst, small.at[i])
        for i, (src, dst) in enumerate(
            ((result_in, result), (igrad_in, igrad), (cond_in, cond))
        )
    ]
    for copy in copies:
        copy.start()
    slots = stage.shape[0]

    def leave(n, _):
        slot, k, t = lax.rem(n, slots), lax.rem(n, 12), 1 - n // 12

        @pl.when(n >= slots)
        def _():
            pltpu.make_async_copy(stage.at[slot], out.at[0], sems.at[slot]).wait()

        def convert(i, _):
            at = pl.ds(pl.multiple_of(i * 128, 128), 128)
            stage[slot, at, :] = w[n, at, :].astype(F32)
            return 0

        lax.fori_loop(0, BLOCK // 128, convert, 0)
        for first, last in ((0, 4), (4, 8), (8, 9), (9, 12)):

            @pl.when((k >= first) & (k < last))
            def _():
                at = pl.ds(pl.multiple_of((k - first) * BLOCK, BLOCK), BLOCK)
                dst = {
                    0: down.at[t, at, :],
                    4: up.at[t, :, at],
                    8: out.at[t],
                    9: qkv.at[t, :, at],
                }[first]
                pltpu.make_async_copy(stage.at[slot], dst, sems.at[slot]).start()

        return 0

    lax.fori_loop(0, 24, leave, 0)
    for slot in range(slots):
        pltpu.make_async_copy(stage.at[slot], out.at[0], sems.at[slot]).wait()
    for copy in copies:
        copy.wait()


def solution(mesh):
    patches = mesh.shape["patch"]

    def shards(nodes, noise, sizes, send, nbr, qkv, out, up, down, cond_w, cot):
        rows, width = nodes.shape[1:]
        halo2 = send.shape[0]
        halo = halo2 // 2
        table = rows + halo2
        freq = np.tile(2.0 ** (np.arange(COND) % (COND // 2) / 4.0), (128, 1)).T.astype(np.float32)
        vmem = pl.BlockSpec(memory_space=pltpu.VMEM)
        hbm = pl.BlockSpec(memory_space=pl.ANY)
        line_bits = (patches // 4).bit_length() - 1
        order = schedule(line_bits, SLOTS)
        stages = 3 + line_bits
        used = [1 + max(v[4] for v in order if v[:3] == ("send", "reduce", s)) for s in range(stages)]
        sems = [1 + max(v[4] for v in order if v[:3] == ("send", "gather", s)) for s in range(stages - 1)]
        boxes = [list(parts) for parts in exchanges(0, 0, 0, [0] * line_bits, False)]
        boxes = [
            (sum(p[2] * p[3][1] for p in parts) // min(BLOCK, parts[0][6][1] * len(parts)), min(BLOCK, parts[0][6][1] * len(parts)))
            for parts in boxes
        ]
        held = pl.pallas_call(
            functools.partial(mega, patches, order),
            out_shape=(
                pltpu.VMEM((1, rows, width), BF16),
                pltpu.VMEM((1, rows, width), F32),
                pltpu.VMEM(cond_w.shape, F32),
                pltpu.VMEM((24, BLOCK, BLOCK), BF16),
            ),
            in_specs=[vmem] * 6 + [hbm] * 6,
            out_specs=(vmem,) * 4,
            scratch_shapes=[
                pltpu.VMEM((table, rows), F32),
                pltpu.VMEM((halo2, rows), BF16),
                pltpu.VMEM((rows, halo2), BF16),
                pltpu.VMEM((8, 1, width), F32),
                pltpu.VMEM((rows, width), F32),
                pltpu.VMEM((rows, width), F32),
                pltpu.VMEM((2, rows, width), F32),
                pltpu.VMEM((2, rows, width), F32),
                pltpu.VMEM((2, rows, 1), F32),
                pltpu.VMEM((2, rows, 1), F32),
                pltpu.VMEM((2, rows, width), BF16),
                pltpu.VMEM((2, rows, width), BF16),
                pltpu.VMEM((rows, width), BF16),
                pltpu.VMEM((width, rows), BF16),
                pltpu.VMEM((2, rows, width), BF16),
                pltpu.VMEM((2, table, 2 * width), BF16),
                pltpu.VMEM((2, HEADS, table, rows), BF16),
                pltpu.VMEM((2, width, rows), BF16),
                pltpu.VMEM((2, 4, rows, BLOCK), BF16),
                pltpu.VMEM((2, 4, rows, BLOCK), BF16),
                pltpu.VMEM((rows, width), BF16),
                pltpu.VMEM((rows, 2 * width), F32),
                pltpu.VMEM((rows, 3 * width), BF16),
                pltpu.VMEM((halo2, 2 * width), BF16),
                pltpu.VMEM((2, halo2, 2 * width), BF16),
                pltpu.VMEM((rows, width), BF16),
                pltpu.VMEM((rows, width), BF16),
                pltpu.VMEM((16, width), F32),
                pltpu.VMEM((8, rows), F32),
                pltpu.VMEM((stages, 16, width), F32),
                pltpu.SemaphoreType.DMA((4,)),
                pltpu.SemaphoreType.DMA((8, 2)),
                pltpu.SemaphoreType.DMA((8, 2)),
                pltpu.SemaphoreType.DMA((stages, max(used))),
                pltpu.SemaphoreType.DMA((stages, max(used))),
                pltpu.SemaphoreType.DMA((stages - 1, max(sems))),
                pltpu.SemaphoreType.DMA((stages - 1, max(sems))),
                pltpu.SemaphoreType.DMA((stages,)),
                pltpu.SemaphoreType.DMA((stages,)),
                pltpu.SemaphoreType.REGULAR((stages,)),
                *(pltpu.VMEM((count, *shape), BF16) for count, shape in zip(used, boxes)),
            ],
            compiler_params=pltpu.CompilerParams(
                collective_id=0, has_side_effects=True, vmem_limit_bytes=49 * 2**20
            ),
        )(noise.reshape(1, 1), sizes.reshape(1, 1), send.reshape(1, -1), nbr, cond_w, freq, nodes, qkv, out, up, down, cot)
        held = [pltpu.with_memory_space_constraint(v, pltpu.VMEM) for v in held]
        result, igrad, cond_grad, *grads = pl.pallas_call(
            widen,
            out_shape=(
                jax.ShapeDtypeStruct((1, rows, width), BF16),
                jax.ShapeDtypeStruct((1, rows, width), F32),
                jax.ShapeDtypeStruct(cond_w.shape, F32),
                *(jax.ShapeDtypeStruct(v.shape, F32) for v in (qkv, out, up, down)),
            ),
            in_specs=[vmem] * 4,
            out_specs=(hbm,) * 7,
            scratch_shapes=[
                pltpu.VMEM((8, BLOCK, BLOCK), F32),
                pltpu.SemaphoreType.DMA((8,)),
                pltpu.SemaphoreType.DMA((3,)),
            ],
            compiler_params=pltpu.CompilerParams(vmem_limit_bytes=32 * 2**20),
        )(*held)
        return (result, igrad, *grads, cond_grad)

    placed = (
        P("noise", "patch", None),
        P("noise"),
        P("patch"),
        P("patch"),
        P(None, "patch"),
        P(),
        P(),
        P(),
        P(),
        P(),
        P("noise", "patch", None),
    )
    return jax.shard_map(
        shards,
        mesh=mesh,
        in_specs=placed,
        out_specs=(P("noise", "patch", None), P("noise", "patch", None), P(), P(), P(), P(), P()),
        check_vma=False,
    )
```

profile of v0, /device:TPU:0, one launch (start us, length us, event | category | flops | bytes accessed | tf_op | source)
XLA Modules:
  0.0 144.0 jit_solution(6598419896582649032)
XLA Ops:
  1.9 132.9 %shard_map.171 = (bf16[1,512,512]{2,1,0:T(8,128)(2,1)S(1)}, f32[1,512,512]{2,1,0:T(8,128)S(1)}, f32[2,4,32,512]{3,2,1,0:T(8,128)S(1)}, bf16[24,512,512]{2,1,0:T(8,128)(2,1)S(1)}) custom-call(f32[1,1]{1,0:T(1,128)} %bitcast.3.noise_ref, s32[1,1]{1,0:T(1,128)} %bitcast.4.sizes_ref, s32[1,128]{1,0:T(1,128)} %bitcast.5, s32[16,512]{1,0:T(8,128)} %nbr_ref.1, ...), custom_call_target="tpu_custom_call" | custom-call | tf_op jit(solution)/shard_map/pallas_call | solution.py:743
  134.8 9.1 %shard_map.172 = (bf16[1,512,512]{2,1,0:T(8,128)(2,1)}, f32[1,512,512]{2,1,0:T(8,128)}, f32[2,4,32,512]{3,2,1,0:T(8,128)}, f32[2,512,1536]{2,1,0:T(8,128)}, f32[...) custom-call(bf16[1,512,512]{2,1,0:T(8,128)(2,1)S(1)} %get-tuple-element.18.result_in, ...), custom_call_target="tpu_custom_call" | custom-call | tf_op jit(solution)/shard_map/pallas_call | solution.py:801
where the time goes:
time: 144 us
  Pallas kernels  142 us (99%)
  between operations  2.12 us (1%)
    pallas_call x1, Pallas kernels, shards(): pl.pallas_call(functools.partial(mega, patches, order), out_shape=(pltpu....  133 us
    pallas_call x1, Pallas kernels, shards(): pl.pallas_call(widen, out_shape=(jax.ShapeDtypeStruct((1, rows, width), B...  9.08 us

commit v1 on v0

--- a/solution.py
+++ b/solution.py
@@ -19,63 +19,52 @@
 BLOCK = 512
 
 
-WHOLE, LEFT, RIGHT = (0, BLOCK), (0, BLOCK // 2), (BLOCK // 2, BLOCK // 2)
-
-
-def square(row, size, x, y, last):
-    one, two = size // 2, size // 4
-    first = [(row + x * one, row + (1 - x) * one, one, LEFT, LEFT, 0, LEFT, "x")]
-    second = []
-    for i in range(2):
-        at = row + i * one
-        first.append((at + y * two, at + (1 - y) * two, two, RIGHT, RIGHT, i * two, RIGHT, "y"))
-        if last:
-            second.append((at + y * two, at + y * two, two, RIGHT, RIGHT, i * two, RIGHT, "x"))
-    mine = row + x * one
-    kept = mine + y * two
-    if last:
-        second.append((mine, mine, one, LEFT, LEFT, 0, LEFT, "y"))
-    else:
-        second.append((kept, mine + (1 - y) * two, two, LEFT, LEFT, 0, LEFT, "y"))
-        other = row + (1 - x) * one + y * two
-        second.append((kept, other, two, RIGHT, RIGHT, 0, RIGHT, "x"))
-    return kept, two, first, second
-
-
-def along_line(row, size, cols, bit, b, last):
-    if last:
-        return (row, size, cols), [(row, row, size, cols, cols, 0, (0, cols[1]), b)]
-    if size >= 32:
-        size //= 2
-        keep, send = row + bit * size, row + (1 - bit) * size
-        return (keep, size, cols), [(keep, send, size, cols, cols, 0, (0, cols[1]), b)]
-    first, width = cols[0], cols[1] // 2
-    keep, send = (first + bit * width, width), (first + (1 - bit) * width, width)
-    return (row, size, keep), [(row, row, size, keep, send, 0, (0, width), b)]
-
-
-def exchanges(core, x, y, bits, line_first):
-    half = BLOCK // 2
-    row, size, cols = core * half, half, WHOLE
-    out = [[(row, (1 - core) * half, half, WHOLE, WHOLE, 0, WHOLE, "core")]]
-    if not line_first:
-        row, size, first, second = square(row, size, x, y, False)
-        out += [first, second]
-    for b, bit in enumerate(bits):
-        last = not line_first and b == len(bits) - 1
-        (row, size, cols), parts = along_line(row, size, cols, bit, b, last)
-        out.append(parts)
-    if line_first:
-        row, size, first, second = square(row, size, x, y, True)
-        out += [first, second]
+def steps(row, cols, side, order, position):
+    size, out = BLOCK // 2, []
+    for d in order:
+        first, width = cols
+        bit = position[d]
+        if d == order[-1]:
+            out.append((row, row, size, cols, cols, 0, (side * width, width), d))
+        elif size >= 32:
+            size //= 2
+            keep, send = row + bit * size, row + (1 - bit) * size
+            out.append((keep, send, size, cols, cols, 0, (side * width, width), d))
+            row = keep
+        else:
+            width //= 2
+            cols, sent = (first + bit * width, width), (first + (1 - bit) * width, width)
+            out.append((row, row, size, cols, sent, 0, (side * width, width), d))
     return out
 
 
-LINE_FIRST = (4, 13, 16, 21)
-
-
-def goes_line_first(n, line_bits):
-    return line_bits == 2 and n in LINE_FIRST
+def exchanges(position, line_bits, flow):
+    half, line = BLOCK // 2, list(range(line_bits))
+    orders = {
+        0: (["x", "y", *line], ["y", "x", *line]),
+        1: (["x", *line, "y"], ["y", *line, "x"]),
+        2: (["x", *line, "y"], ["y", "x", *line]),
+        3: (["x", "y", *line], ["y", *line, "x"]),
+        4: ([*line, "x", "y"], [*line, "y", "x"]),
+    }[flow]
+    row, other = position["core"] * half, (1 - position["core"]) * half
+    cols = (0, BLOCK)
+    out = [[(row, other, half, cols, cols, 0, cols, "core")]]
+    left = steps(row, (0, half), 0, orders[0], position)
+    right = steps(row, (half, half), 1, orders[1], position)
+    return out + [list(both) for both in zip(left, right)]
+
+
+FLOWS = (0, 0, 0, 0, 0, 4, 0, 0, 0, 0, 0, 0, 0, 4, 0, 0, 0, 0, 4, 0, 0, 4, 0, 0)
+
+
+def plans_for(position, line_bits):
+    made = {f: exchanges(position, line_bits, f) for f in (set(FLOWS) if line_bits == 2 else {0})}
+    return [made[FLOWS[n] if line_bits == 2 else 0] for n in range(24)]
+
+
+def nowhere(line_bits):
+    return dict.fromkeys(["core", "x", "y", *range(line_bits)], 0)
 
 
 MADE = {
@@ -85,32 +74,44 @@
 }
 LAYER_PIECES = (
     (
-        "down0", "down1", "feed0", "down2", "feed1", "down3", "feed2", "feed3", "up0", "norm2", "attended",
-        "up3", "head0", "up1", "head1", "halo0", "head2", "head3", "halo1", "up2", "out", "query", "table",
+        "down0", "feed0", "down1", "feed1", "down2", "feed2", "down3", "feed3", "norm2", "up0", "attended",
+        "head0", "up1", "head1", "head2", "halo0", "up2", "head3", "halo1", "up3", "query", "out", "table",
         "key", "value", "norm1",
     ),
     (
-        "down0", "down1", "down2", "feed0", "feed1", "feed2", "down3", "feed3", "norm2", "up2", "attended",
-        "head0", "up1", "head1", "halo0", "up0", "head2", "head3", "up3", "halo1", "query", "out", "table",
-        "key", "value", "norm1",
+        "down0", "feed0", "down1", "up0", "down2", "down3", "feed1", "feed2", "feed3", "norm2", "up1",
+        "attended", "up3", "head0", "head1", "up2", "halo0", "head2", "head3", "halo1", "out", "query",
+        "table", "key", "value", "norm1",
     ),
 )
 
-REDUCE_LAGS = ((1, 3, 2, 3, 4), (1, 4, 4, 3, 2))
-GATHER_LAGS = ((3, 3, 7, 3), (2, 4, 7, 5))
-GATHER_WAIT = (1, 1)
+REDUCE_LAGS = (
+    (1, 3, 3, 3, 3),
+    (1, 3, 3, 3, 3),
+    (1, 3, 3, 3, 3),
+    (1, 3, 2, 3, 4),
+    (1, 3, 3, 2, 4),
+)
+GATHER_LAGS = (
+    (3, 4, 9, 4),
+    (3, 4, 8, 5),
+    (3, 4, 8, 5),
+    (3, 4, 8, 5),
+    (5, 3, 7, 11),
+)
+GATHER_WAIT = (1, 1, 1, 1, 1)
 SUMS_LAG = 3
 
 
 def schedule(line_bits, slots):
-    tables = [exchanges(0, 0, 0, [0] * line_bits, f) for f in (False, True)]
+    tables = plans_for(nowhere(line_bits), line_bits)
     stages = 3 + line_bits
     sum_dirs = ["core", "x", *range(line_bits), "y"]
 
     def dirs_of(kind, s, n):
         if kind == "sums":
             return {sum_dirs[s]}
-        return {p[7] for p in tables[goes_line_first(n, line_bits)][s]}
+        return {p[7] for p in tables[n][s]}
 
     order, sent, seen = [], [], set()
     reduced = {}
@@ -131,7 +132,7 @@
     def lag(kind, s, n):
         if kind == "sums":
             return SUMS_LAG
-        lags = (REDUCE_LAGS if kind == "reduce" else GATHER_LAGS)[goes_line_first(n, line_bits)]
+        lags = (REDUCE_LAGS if kind == "reduce" else GATHER_LAGS)[FLOWS[n]]
         if kind == "reduce":
             return lags[min(s, len(lags) - 1)]
         return lags[max(0, len(lags) - 1 - s)]
@@ -168,7 +169,7 @@
                 if s + 1 < stages:
                     waiting.append((turn, kind, s + 1, n))
                 else:
-                    wait = GATHER_WAIT[goes_line_first(n, line_bits)]
+                    wait = GATHER_WAIT[FLOWS[n]]
                     waiting.append((turn + wait, "gather", s - 1, n))
             elif kind == "gather" and s > 0:
                 waiting.append((turn, kind, s - 1, n))
@@ -213,6 +214,7 @@
 def mega(
     patches,
     order,
+    first_sem,
     noise_ref,
     sizes_ref,
     send_ref,
@@ -258,14 +260,13 @@
     cot_in,
     sums,
     stat,
+    fade,
     sums_in,
     load_sem,
     halo_send,
     halo_recv,
-    rs_send,
-    rs_recv,
-    ag_send,
-    ag_recv,
+    block_send,
+    block_recv,
     sum_send,
     sum_recv,
     token,
@@ -290,10 +291,10 @@
 
     def load(t, k):
         src = place(t, k, down_hbm, up_hbm, out_hbm, qkv_hbm)
-        return pltpu.make_async_copy(src, w.at[(1 - t) * 12 + k], load_sem.at[t])
-
-    node_copy = pltpu.make_async_copy(nodes_hbm.at[0], node_in, load_sem.at[2])
-    cot_copy = pltpu.make_async_copy(cot_hbm.at[0], cot_in, load_sem.at[3])
+        return pltpu.make_async_copy(src, w.at[(1 - t) * 12 + k], load_sem.at[t, k // 8])
+
+    node_copy = pltpu.make_async_copy(nodes_hbm.at[0], node_in, load_sem.at[2, 0])
+    cot_copy = pltpu.make_async_copy(cot_hbm.at[0], cot_in, load_sem.at[2, 1])
     node_copy.start()
     for t in range(2):
         for k in (9, 10, 11, 8, 4, 0, 5, 1, 6, 2, 7, 3):
@@ -369,7 +370,7 @@
             ).astype(BF16)
             return 0
 
-        lax.fori_loop(0, rows // ln_rows, body, 0, unroll=4)
+        lax.fori_loop(0, rows // ln_rows, body, 0, unroll=8)
 
     def halo_copies(stage, part, src, dst, to_before, to_after):
         cols = pl.ds(part * BLOCK, BLOCK)
@@ -387,9 +388,9 @@
 
     def forward(t, _):
         base = (1 - t) * 12
-        layer = w.at[pl.ds(base, 12)]
-        pltpu.make_async_copy(layer, layer, load_sem.at[t]).wait()
         norm(hid, t, 0, xh1, rs1, act1)
+        loaded = w.at[pl.ds(base + 8, 4)]
+        pltpu.make_async_copy(loaded, loaded, load_sem.at[t, 1]).wait()
         a = act1[t]
         copies = []
         for part in range(2):
@@ -411,6 +412,7 @@
                 prob[t, h, own, cols] = part.astype(BF16)
                 stat[2 * h : 2 * h + 1, cols] = top
                 stat[2 * h + 1 : 2 * h + 2, cols] = jnp.sum(part, 0, keepdims=True)
+            mid[lanes, :] = tn(kv[t, own, pl.ds(BLOCK + h * head, head)], prob[t, h, own, :])
         for copy in copies[0]:
             copy.wait()
         for h in range(HEADS):
@@ -422,15 +424,18 @@
             scale = jnp.exp2(near_top - top)
             inv = 1.0 / (stat[2 * h + 1 : 2 * h + 2, :] * scale + jnp.sum(part, 0, keepdims=True))
             prob[t, h, far, :] = (part * inv).astype(BF16)
-            prob[t, h, own, :] = (prob[t, h, own, :].astype(F32) * (scale * inv)).astype(BF16)
+            fade[t, h : h + 1, :] = scale * inv
         for copy in copies[1]:
             copy.wait()
         for h in range(HEADS):
             lanes = pl.ds(h * head, head)
-            values = kv[t, :, pl.ds(BLOCK + h * head, head)]
-            att_t[t, lanes, :] = tn(values, prob[t, h]).astype(BF16)
+            near = mid[lanes, :] * fade[t, h : h + 1, :]
+            values = kv[t, far, pl.ds(BLOCK + h * head, head)]
+            att_t[t, lanes, :] = (near + tn(values, prob[t, h, far, :])).astype(BF16)
         mid[...] = hid[...] + tn(att_t[t], w[base + 8])
         norm(mid, t, 2, xh2, rs2, act2)
+        loaded = w.at[pl.ds(base, 8)]
+        pltpu.make_async_copy(loaded, loaded, load_sem.at[t, 0]).wait()
         for f in range(4):
             u = nn(act2[t], w[base + 4 + f])
             sig = 0.5 * jnp.tanh(0.5 * u) + 0.5
@@ -452,10 +457,12 @@
         ids = lax.broadcasted_iota(jnp.int32, (ln_rows, hid.shape[1]), 0) + i * ln_rows
         live = ids < sizes_ref[...]
         result_ref[0, at, :] = jnp.where(live, hid[at, :], 0.0).astype(BF16)
-        hid[at, :] = jnp.where(live, cot_in[at, :].astype(F32), 0.0)
+        start = jnp.where(live, cot_in[at, :].astype(F32), 0.0)
+        hid[at, :] = start
+        low[at, :] = start.astype(BF16)
         return 0
 
-    lax.fori_loop(0, rows // ln_rows, turn, 0)
+    lax.fori_loop(0, rows // ln_rows, turn, 0, unroll=8)
 
     def norm_back(t, first, grad_ref, normed_ref, inv_ref, add_ref, out_ref):
         def body(i, carry):
@@ -481,13 +488,14 @@
 
     bits = [lax.rem(z // (1 << b), 2) for b in range(line.bit_length() - 1)]
     stages = 3 + len(bits)
-    plans = [exchanges(core, x, y, bits, f) for f in (False, True)]
+    position = {"core": core, "x": x, "y": y, **dict(enumerate(bits))}
+    plans = plans_for(position, len(bits))
     peers = {"core": core_peer, "x": x_peer, "y": y_peer}
     for b, bit in enumerate(bits):
         peers[b] = (my_noise, me + 4 * (1 << b) * (1 - 2 * bit))
 
     def parts_of(s, n):
-        return plans[goes_line_first(n, len(bits))][s]
+        return plans[n][s]
 
     def box(row, size, cols):
         at = pl.ds(row if isinstance(row, int) else pl.multiple_of(row, 16), size)
@@ -505,9 +513,8 @@
         ).start()
 
     def pair_of(kind, s, slot):
-        if kind == "reduce":
-            return rs_send.at[s, slot], rs_recv.at[s, slot]
-        return ag_send.at[s, slot], ag_recv.at[s, slot]
+        at = first_sem[kind, s] + slot
+        return block_send.at[at], block_recv.at[at]
 
     def send_block(kind, s, n, slot):
         pair = pair_of(kind, s, slot)
@@ -528,12 +535,12 @@
         settle(inbox[s].at[slot if kind == "reduce" else 0], pair_of(kind, s, slot))
         if kind == "reduce":
             for keep, _, size, cols, _, at, at_cols, _ in parts_of(s, n):
-                step = min(size, 32)
+                step = min(size, 64)
 
                 def add(i, _, keep=keep, cols=cols, at=at, at_cols=at_cols, step=step):
                     mine = (n, *box(keep + i * step, step, cols))
                     got = inbox[s][slot, *box(at + i * step, step, at_cols)]
-                    w[mine] = (w[mine].astype(F32) + got.astype(F32)).astype(BF16)
+                    w[mine] = w[mine] + got
                     return 0
 
                 lax.fori_loop(0, size // step, add, 0)
@@ -551,8 +558,6 @@
         settle(sums_in.at[s, sum_rows(s)], (sum_send.at[s], sum_recv.at[s]))
         if s + 1 < len(sum_dirs):
             sums[0:8, :] = sums[0:8, :] + sums_in[s, 0:8, :]
-
-    low[...] = hid[...].astype(BF16)
 
     def pieces_of(i):
         t = 1 - i
@@ -580,12 +585,14 @@
             lanes = pl.ds(h * head, head)
             keys = kv[t, :, lanes]
             values = kv[t, :, pl.ds(BLOCK + h * head, head)]
-            weight = prob[t, h]
+            near = prob[t, h, pl.ds(0, rows), :].astype(F32) * fade[t, h : h + 1, :]
+            share = jnp.concatenate([near, prob[t, h, pl.ds(rows, table - rows), :].astype(F32)], 0)
+            weight = share.astype(BF16)
             grad_out = dob[:, lanes]
             grad_weight = nt(values, grad_out)
-            spread = weight.astype(F32) * grad_weight
+            spread = share * grad_weight
             delta = jnp.sum(spread, 0, keepdims=True)
-            ds = (spread - weight.astype(F32) * delta).astype(BF16)
+            ds = (spread - share * delta).astype(BF16)
             dv = nn(weight, grad_out)
             dk = nn(ds, qv[t, :, lanes]) * (head ** (-0.5))
             dq_t = tn(keys, ds) * (head ** (-0.5))
@@ -641,8 +648,18 @@
         work["table"] = whole_table
         work["key"] = functools.partial(project, 1)
         work["value"] = functools.partial(project, 2)
-        work["norm1"] = functools.partial(norm_back, t, 0, hid, xh1, rs1, mid, hid)
+        work["norm1"] = functools.partial(
+            norm_back, t, 0, hid, xh1, rs1, mid, hid if i == 0 else igrad_ref.at[0]
+        )
         return work
+
+    def cond_gradient():
+        far_sums = len(sum_dirs) - 1
+        other = features(jnp.concatenate([sums_in[far_sums, 8:16, 0:128]] * (COND // 8), axis=0))
+        for t in range(2):
+            for i in range(4):
+                row = pl.ds(t * 4 + i, 1)
+                cond_grad_ref[t, i] = wide * sums[row, :] + other * sums_in[far_sums, row, :]
 
     layers = [pieces_of(0), pieces_of(1)]
     for act, *rest in order:
@@ -653,6 +670,8 @@
             kind, s, n, slot = rest
             if kind == "sums":
                 (send_sums if act == "send" else take_sums)(s)
+                if act == "take" and s == len(sum_dirs) - 1:
+                    cond_gradient()
             elif kind == "token":
                 if act == "send":
                     told = token.at[s if isinstance(s, int) else len(bits) + "xyc".index(s[0])]
@@ -661,14 +680,6 @@
                     pl.semaphore_wait(told, 1)
             else:
                 (send_block if act == "send" else take_block)(kind, s, n, slot)
-
-    igrad_ref[0] = hid[...]
-    far_sums = len(sum_dirs) - 1
-    other = features(jnp.concatenate([sums_in[far_sums, 8:16, 0:128]] * (COND // 8), axis=0))
-    for t in range(2):
-        for i in range(4):
-            row = pl.ds(t * 4 + i, 1)
-            cond_grad_ref[t, i] = wide * sums[row, :] + other * sums_in[far_sums, row, :]
 
 
 def widen(
@@ -733,15 +744,21 @@
         line_bits = (patches // 4).bit_length() - 1
         order = schedule(line_bits, SLOTS)
         stages = 3 + line_bits
-        used = [1 + max(v[4] for v in order if v[:3] == ("send", "reduce", s)) for s in range(stages)]
-        sems = [1 + max(v[4] for v in order if v[:3] == ("send", "gather", s)) for s in range(stages - 1)]
-        boxes = [list(parts) for parts in exchanges(0, 0, 0, [0] * line_bits, False)]
+        counts = {}
+        for act, kind, s, *slot in order:
+            if act == "send" and kind in ("reduce", "gather"):
+                counts[kind, s] = max(counts.get((kind, s), 0), slot[1] + 1)
+        first_sem, total = {}, 0
+        for key, count in counts.items():
+            first_sem[key] = total
+            total += count
+        boxes = [list(parts) for parts in plans_for(nowhere(line_bits), line_bits)[0]]
         boxes = [
             (sum(p[2] * p[3][1] for p in parts) // min(BLOCK, parts[0][6][1] * len(parts)), min(BLOCK, parts[0][6][1] * len(parts)))
             for parts in boxes
         ]
         held = pl.pallas_call(
-            functools.partial(mega, patches, order),
+            functools.partial(mega, patches, order, first_sem),
             out_shape=(
                 pltpu.VMEM((1, rows, width), BF16),
                 pltpu.VMEM((1, rows, width), F32),
@@ -780,18 +797,17 @@
                 pltpu.VMEM((rows, width), BF16),
                 pltpu.VMEM((16, width), F32),
                 pltpu.VMEM((8, rows), F32),
+                pltpu.VMEM((2, 8, rows), F32),
                 pltpu.VMEM((stages, 16, width), F32),
-                pltpu.SemaphoreType.DMA((4,)),
+                pltpu.SemaphoreType.DMA((3, 2)),
                 pltpu.SemaphoreType.DMA((8, 2)),
                 pltpu.SemaphoreType.DMA((8, 2)),
-                pltpu.SemaphoreType.DMA((stages, max(used))),
-                pltpu.SemaphoreType.DMA((stages, max(used))),
-                pltpu.SemaphoreType.DMA((stages - 1, max(sems))),
-                pltpu.SemaphoreType.DMA((stages - 1, max(sems))),
+                pltpu.SemaphoreType.DMA((sum(counts.values()),)),
+                pltpu.SemaphoreType.DMA((sum(counts.values()),)),
                 pltpu.SemaphoreType.DMA((stages,)),
                 pltpu.SemaphoreType.DMA((stages,)),
                 pltpu.SemaphoreType.REGULAR((stages,)),
-                *(pltpu.VMEM((count, *shape), BF16) for count, shape in zip(used, boxes)),
+                *(pltpu.VMEM((count, *shape), BF16) for count, shape in zip((counts["reduce", s] for s in range(stages)), boxes)),
             ],
             compiler_params=pltpu.CompilerParams(
                 collective_id=0, has_side_effects=True, vmem_limit_bytes=49 * 2**20

time: 144 us -> 140 us (0.972)
  Pallas kernels: 142 us -> 138 us
    pallas_call x1, Pallas kernels: 133 us -> 129 us  [shards(): pl.pallas_call(functools.partial(mega, patches, order, first_sem), out_sh...]
where the time goes in v1:
time: 140 us
  Pallas kernels  138 us (99%)
  between operations  2.12 us (2%)
    pallas_call x1, Pallas kernels, shards(): pl.pallas_call(functools.partial(mega, patches, order, first_sem), out_sh...  129 us
    pallas_call x1, Pallas kernels, shards(): pl.pallas_call(widen, out_shape=(jax.ShapeDtypeStruct((1, rows, width), B...  9.08 us

profile of v1, /device:TPU:0, one launch (start us, length us, event | category | flops | bytes accessed | tf_op | source)
XLA Modules:
  0.0 139.8 jit_solution(3340467935353518604)
XLA Ops:
  1.9 128.6 %shard_map.171 = (bf16[1,512,512]{2,1,0:T(8,128)(2,1)S(1)}, f32[1,512,512]{2,1,0:T(8,128)S(1)}, f32[2,4,32,512]{3,2,1,0:T(8,128)S(1)}, bf16[24,512,512]{2,1,0:T(8,128)(2,1)S(1)}) custom-call(f32[1,1]{1,0:T(1,128)} %bitcast.3.noise_ref, s32[1,1]{1,0:T(1,128)} %bitcast.4.sizes_ref, s32[1,128]{1,0:T(1,128)} %bitcast.5, s32[16,512]{1,0:T(8,128)} %nbr_ref.1, ...), custom_call_target="tpu_custom_call" | custom-call | tf_op jit(solution)/shard_map/pallas_call | solution.py:760
  130.5 9.1 %shard_map.172 = (bf16[1,512,512]{2,1,0:T(8,128)(2,1)}, f32[1,512,512]{2,1,0:T(8,128)}, f32[2,4,32,512]{3,2,1,0:T(8,128)}, f32[2,512,1536]{2,1,0:T(8,128)}, f32[...) custom-call(bf16[1,512,512]{2,1,0:T(8,128)(2,1)S(1)} %get-tuple-element.18.result_in, ...), custom_call_target="tpu_custom_call" | custom-call | tf_op jit(solution)/shard_map/pallas_call | solution.py:817

commit v2 on v1

--- a/solution.py
+++ b/solution.py
@@ -156,7 +156,7 @@
 
     def take_turn(turn):
         due = [v for v in flying if v[0] <= turn]
-        rank = {"gather": 0, "sums": 1, "reduce": 2}
+        rank = {"reduce": 0, "sums": 1, "gather": 2}
         due.sort(key=lambda v: (rank[v[1]], v[2] if v[1] == "gather" else -v[2], v[3]))
         for item in due:
             flying.remove(item)
@@ -220,7 +220,6 @@
     send_ref,
     nbr_ref,
     cond_w_ref,
-    freq_ref,
     nodes_hbm,
     qkv_hbm,
     out_hbm,
@@ -337,8 +336,12 @@
     sel[...] = picked.T.astype(BF16)
 
     def features(noise):
-        phase = jnp.log(noise) * freq_ref[...]
-        is_sin = lax.broadcasted_iota(jnp.int32, (COND, 128), 0) < COND // 2
+        row = lax.broadcasted_iota(jnp.int32, (COND, 128), 0)
+        is_sin = row < COND // 2
+        frequency = jnp.full((COND, 128), 1.0, F32)
+        for i in range(1, COND // 2):
+            frequency = jnp.where(row % (COND // 2) == i, np.float32(2.0 ** (i / 4)), frequency)
+        phase = jnp.log(noise) * frequency
         feats = jnp.where(is_sin, jnp.sin(phase), jnp.cos(phase))
         return jnp.concatenate([feats] * (hid.shape[1] // 128), axis=1)
 
@@ -707,7 +710,7 @@
             stage[slot, at, :] = w[n, at, :].astype(F32)
             return 0
 
-        lax.fori_loop(0, BLOCK // 128, convert, 0)
+        lax.fori_loop(0, BLOCK // 128, convert, 0, unroll=4)
         for first, last in ((0, 4), (4, 8), (8, 9), (9, 12)):
 
             @pl.when((k >= first) & (k < last))
@@ -738,7 +741,6 @@
         halo2 = send.shape[0]
         halo = halo2 // 2
         table = rows + halo2
-        freq = np.tile(2.0 ** (np.arange(COND) % (COND // 2) / 4.0), (128, 1)).T.astype(np.float32)
         vmem = pl.BlockSpec(memory_space=pltpu.VMEM)
         hbm = pl.BlockSpec(memory_space=pl.ANY)
         line_bits = (patches // 4).bit_length() - 1
@@ -765,7 +767,7 @@
                 pltpu.VMEM(cond_w.shape, F32),
                 pltpu.VMEM((24, BLOCK, BLOCK), BF16),
             ),
-            in_specs=[vmem] * 6 + [hbm] * 6,
+            in_specs=[vmem] * 5 + [hbm] * 6,
             out_specs=(vmem,) * 4,
             scratch_shapes=[
                 pltpu.VMEM((table, rows), F32),
@@ -812,7 +814,7 @@
             compiler_params=pltpu.CompilerParams(
                 collective_id=0, has_side_effects=True, vmem_limit_bytes=49 * 2**20
             ),
-        )(noise.reshape(1, 1), sizes.reshape(1, 1), send.reshape(1, -1), nbr, cond_w, freq, nodes, qkv, out, up, down, cot)
+        )(noise.reshape(1, 1), sizes.reshape(1, 1), send.reshape(1, -1), nbr, cond_w, nodes, qkv, out, up, down, cot)
         held = [pltpu.with_memory_space_constraint(v, pltpu.VMEM) for v in held]
         result, igrad, cond_grad, *grads = pl.pallas_call(
             widen,
@@ -825,8 +827,8 @@
             in_specs=[vmem] * 4,
             out_specs=(hbm,) * 7,
             scratch_shapes=[
-                pltpu.VMEM((8, BLOCK, BLOCK), F32),
-                pltpu.SemaphoreType.DMA((8,)),
+                pltpu.VMEM((12, BLOCK, BLOCK), F32),
+                pltpu.SemaphoreType.DMA((12,)),
                 pltpu.SemaphoreType.DMA((3,)),
             ],
             compiler_params=pltpu.CompilerParams(vmem_limit_bytes=32 * 2**20),

time: 140 us -> 140 us (level)
  no operation moved by 1% of the time
where the time goes in v2:
time: 140 us
  Pallas kernels  138 us (99%)
  between operations  2.12 us (2%)
    pallas_call x1, Pallas kernels, shards(): pl.pallas_call(functools.partial(mega, patches, order, first_sem), out_sh...  129 us
    pallas_call x1, Pallas kernels, shards(): pl.pallas_call(widen, out_shape=(jax.ShapeDtypeStruct((1, rows, width), B...  9.11 us

profile of v2, /device:TPU:0, one launch (start us, length us, event | category | flops | bytes accessed | tf_op | source)
XLA Modules:
  0.0 139.8 jit_solution(3791497633185545184)
XLA Ops:
  1.9 128.6 %shard_map.162 = (bf16[1,512,512]{2,1,0:T(8,128)(2,1)S(1)}, f32[1,512,512]{2,1,0:T(8,128)S(1)}, f32[2,4,32,512]{3,2,1,0:T(8,128)S(1)}, bf16[24,512,512]{2,1,0:T(8,128)(2,1)S(1)}) custom-call(f32[1,1]{1,0:T(1,128)} %bitcast.3.noise_ref, s32[1,1]{1,0:T(1,128)} %bitcast.4.sizes_ref, s32[1,128]{1,0:T(1,128)} %bitcast.5, s32[16,512]{1,0:T(8,128)} %nbr_ref.1, ...), custom_call_target="tpu_custom_call" | custom-call | tf_op jit(solution)/shard_map/pallas_call | solution.py:762
  130.5 9.1 %shard_map.163 = (bf16[1,512,512]{2,1,0:T(8,128)(2,1)}, f32[1,512,512]{2,1,0:T(8,128)}, f32[2,4,32,512]{3,2,1,0:T(8,128)}, f32[2,512,1536]{2,1,0:T(8,128)}, f32[...) custom-call(bf16[1,512,512]{2,1,0:T(8,128)(2,1)S(1)} %get-tuple-element.18.result_in, ...), custom_call_target="tpu_custom_call" | custom-call | tf_op jit(solution)/shard_map/pallas_call | solution.py:819
